TPU v7x, 32 devices: a whole 2x2x4 slice. The times are simulated.
32 devices in a mesh: seq: 4 (over y, x), head: 8 (over z, core).
Axes of the slice: x: 2, y: 2, z: 4, core: 2. Of those that a mesh axis runs over, the one named last changes fastest.
Arguments:
- out_grad: bfloat16 [2048, 8192], P('seq'), may hold values from -6 to 6
- out_weight: bfloat16 [8192, 8192], P(None, 'head'), may hold values from -0.0625 to 0.0625
- gate_input: bfloat16 [2048, 8192], P('seq', 'head'), may hold values from -6 to 6
- scan_output: bfloat16 [2048, 8192], P('seq', 'head'), may hold values from -6 to 6
- step_size: float32 [2048, 128], P('seq', 'head'), may hold values from 0.5 to 2
- log_decay: float32 [2048, 128], P('seq', 'head'), may hold values from -1 to 0
- input_map: bfloat16 [2048, 4, 256], P('seq'), may hold values from -0.375 to 0.375
- output_map: bfloat16 [2048, 4, 256], P('seq'), may hold values from -0.375 to 0.375
- skip_gain: float32 [128], P('head'), may hold values from 0.5 to 1.5
Outputs:
- input_grad: bfloat16 [2048, 8192], P('seq', 'head')
- gate_grad: bfloat16 [2048, 8192], P('seq', 'head')
- weight_grad: bfloat16 [8192, 8192], P(None, 'head')
All inputs are finite; a program needn't handle non-finite values.
Results may differ from a plain program's by a relative error of at most 0.02.
Values may be sent and summed in bfloat16 or wider, within the bound.
A program may use at most 192 MiB of HBM per device.

v0:
```python
import math

import jax
import jax.numpy as jnp
from jax import lax
from jax.experimental import pallas as pl
from jax.experimental.pallas import tpu as pltpu
from jax.sharding import PartitionSpec as P

HEAD_COUNT = 128
G = 4
SUB = 128

f32 = jnp.float32
bf16 = jnp.bfloat16
highest = lax.Precision.HIGHEST
MESH = pl.DeviceIdType.MESH


def gate_terms(gate_input, scan_output):
    gate_value = gate_input.astype(f32)
    sig = jax.nn.sigmoid(gate_value)
    silu = gate_value * sig
    saved = scan_output.astype(f32)
    slope = saved * sig * (1.0 + gate_value * (1.0 - sig))
    gated = (saved * silu).astype(bf16)
    return silu, slope, gated


def spread_heads(values, width):
    heads = values.shape[1]
    owner = jnp.arange(heads * width) // width
    expand = (owner[None, :] == jnp.arange(heads)[:, None]).astype(f32)
    return jnp.dot(values, expand, precision=highest, preferred_element_type=f32)


def scan_pieces(scan_grad, cumulative, in_group, out_group):
    length, heads = cumulative.shape
    width = scan_grad.shape[1] // heads
    chunks = length // SUB
    grad_float = scan_grad.astype(f32)
    weighted = (grad_float * spread_heads(jnp.exp(cumulative), width)).astype(bf16)
    local_state = jnp.einsum("tk,tn->kn", weighted, out_group, preferred_element_type=f32)

    ends = cumulative[SUB - 1 :: SUB]
    b_c = in_group.reshape(chunks, SUB, -1)
    c_c = out_group.reshape(chunks, SUB, -1)
    scores = jnp.einsum("ctn,csn->cts", b_c, c_c, preferred_element_type=f32)
    cum_c = cumulative.reshape(chunks, SUB, heads).transpose(0, 2, 1)
    spread = cum_c[:, :, None, :] - cum_c[:, :, :, None]
    pos = jnp.arange(SUB)
    mask = pos[:, None] <= pos[None, :]
    factor = jnp.where(mask, jnp.exp(jnp.minimum(spread, 0.0)), 0.0)
    weights = (scores[:, None] * factor).astype(bf16)
    grads = scan_grad.reshape(chunks, SUB, heads, width)
    inside = jnp.einsum("chts,cshp->cthp", weights, grads, preferred_element_type=f32)
    inside = inside.reshape(length, heads * width)
    state = None
    later = [jnp.zeros((SUB, heads * width), f32)]
    for j in range(chunks - 2, -1, -1):
        rows = slice((j + 1) * SUB, (j + 2) * SUB)
        decay = spread_heads(jnp.exp(cumulative[rows] - ends[j][None]), width)
        fresh = jnp.einsum(
            "tn,tk->nk",
            out_group[rows],
            (grad_float[rows] * decay).astype(bf16),
            preferred_element_type=f32,
        )
        state = fresh if state is None else fresh + decay[-1][None] * state
        seen = jnp.dot(
            in_group[j * SUB : (j + 1) * SUB], state.astype(bf16), preferred_element_type=f32
        )
        tail = spread_heads(jnp.exp(ends[j][None] - cumulative[j * SUB : (j + 1) * SUB]), width)
        later.insert(0, seen * tail)
    return local_state, inside + jnp.concatenate(later, axis=0)


def group_maps(input_map, output_map, heads_here):
    index = lax.axis_index("head") * heads_here // (HEAD_COUNT // G)
    pick = lambda m: lax.dynamic_index_in_dim(m, index, 1, keepdims=False)
    return pick(input_map), pick(output_map)


def finish(inside, carried, scan_grad, cumulative, in_group, step_size, skip_gain):
    heads = cumulative.shape[1]
    width = scan_grad.shape[1] // heads
    seen = jnp.einsum("tn,kn->tk", in_group, carried.astype(bf16), preferred_element_type=f32)
    tail = spread_heads(jnp.exp(cumulative[-1:] - cumulative), width)
    return (
        spread_heads(step_size, width) * (inside + tail * seen)
        + jnp.repeat(skip_gain, width)[None] * scan_grad.astype(f32)
    ).astype(bf16)


def general(
    out_grad,
    out_weight,
    gate_input,
    scan_output,
    step_size,
    log_decay,
    input_map,
    output_map,
    skip_gain,
):
    length = out_grad.shape[0]
    heads_here = log_decay.shape[1]
    n_seq = lax.axis_size("seq")
    width = gate_input.shape[1] // heads_here
    cols = out_weight.shape[1]
    silu, slope, gated = gate_terms(gate_input, scan_output)
    mine = lax.dynamic_slice_in_dim(out_grad, lax.axis_index("head") * cols, cols, 1)
    row_panel = lax.all_to_all(out_weight, "head", split_axis=0, concat_axis=1, tiled=True)
    upstream = jnp.einsum("td,kd->tk", out_grad, row_panel, preferred_element_type=f32)
    gate_grad = (upstream * slope).astype(bf16)
    scan_grad = (upstream * silu).astype(bf16)
    in_group, out_group = group_maps(input_map, output_map, heads_here)
    cumulative = jnp.cumsum(log_decay, axis=0)
    local_state, inside = scan_pieces(scan_grad, cumulative, in_group, out_group)
    decay_all = jnp.repeat(jnp.exp(cumulative[-1]), width)[:, None]

    def relay_turn(_, carried_in):
        outgoing = (local_state + decay_all * carried_in).astype(bf16)
        route = [(i + 1, i) for i in range(n_seq - 1)]
        return lax.ppermute(outgoing, "seq", route).astype(f32)

    carried = lax.fori_loop(0, n_seq - 1, relay_turn, jnp.zeros_like(local_state))
    input_grad = finish(inside, carried, scan_grad, cumulative, in_group, step_size, skip_gain)
    gated_all = lax.all_gather(gated, "head", axis=1, tiled=True)
    part = jnp.einsum("tk,td->kd", gated_all, mine, preferred_element_type=f32)
    part = (part * (1.0 / math.sqrt(length * n_seq))).astype(bf16)
    return input_grad, gate_grad, lax.psum(part, "seq")


def mirror(at, upper):
    return at + upper * (3 - 2 * at)


def exchange(
    out_grad,
    out_weight,
    gated_t,
    gate_input,
    scan_output,
    in_group,
    out_group_t,
    factors,
    cumul,
    cumul_t,
    expand,
    skip,
    weight_grad,
    gate_grad,
    input_grad,
    cls,
    og,
    wbuf,
    xsend,
    xrecv,
    xsum,
    rs,
    st_own,
    st_x,
    st_pair,
    st_y,
    total,
    total_x,
    inside,
    state,
    local_sem,
    w_sem,
    xs,
    xr,
    rss,
    rsr,
    zs,
    zr,
    es,
    er,
    bs,
    br,
    cs,
    cr,
    ks,
    kr,
    ts,
    tr,
    ol,
    os_,
    or_,
):
    cols, length = gated_t.shape
    tile = min(256, cols)
    tiles = cols // tile
    s, h = lax.axis_index("seq"), lax.axis_index("head")
    z, core = lax.div(h, 2), lax.rem(h, 2)
    upper = lax.div(z, 2)
    zz = z + upper * (3 - 2 * z)
    inner, end = zz == 1, zz == 0
    mate = h + 1 - 2 * core
    dev_core = (s, mate)
    dev_x = (s + 1 - 2 * lax.rem(s, 2), h)
    dev_y = (lax.rem(s + 2, 4), h)
    inward = mirror(zz + 1, upper)
    dev_in = (s, inward * 2 + core)
    dev_out = (s, mirror(0, upper) * 2 + core)
    seg = [mirror(3, upper), mirror(2, upper), mirror(1 - zz, upper), z]
    plane = [z, inward, mirror(2 - 2 * zz, upper), mirror(3, upper)]

    def remote(src, dst, ssem, rsem, dev):
        return pltpu.make_async_remote_copy(
            src_ref=src, dst_ref=dst, send_sem=ssem, recv_sem=rsem, device_id=dev, device_id_type=MESH
        )

    heads = cumul.shape[1]
    width = cols // heads
    sub = length // 4

    def spread(values):
        return jnp.dot(values, expand[...], precision=highest, preferred_element_type=f32)

    def own_cols(part, sem):
        who = h if part == 0 else mate
        return pltpu.make_async_copy(
            out_grad.at[:, pl.ds(pl.multiple_of(who * cols, cols), cols)],
            og.at[pl.ds(0, length), pl.ds(part * cols, cols)],
            local_sem.at[sem],
        )

    def w_load(i):
        who = (1 - core) if i % 2 == 0 else core
        row = pl.multiple_of((seg[i // 2] * 2 + who) * cols, cols)
        return pltpu.make_async_copy(
            out_weight.at[pl.ds(row, cols), :], wbuf.at[i % 2], w_sem.at[i % 2]
        )

    own_cols(0, 0).start()
    own_cols(1, 1).start()
    w_load(0).start()
    w_load(1).start()

    barrier = pltpu.get_barrier_semaphore()
    for dev in (dev_core, dev_x, dev_y, dev_in):
        pl.semaphore_signal(barrier, inc=1, device_id=dev, device_id_type=MESH)

    @pl.when(inner)
    def _():
        pl.semaphore_signal(barrier, inc=1, device_id=dev_out, device_id_type=MESH)

    @pl.when(inner)
    def _():
        pl.semaphore_wait(barrier, 5)

    @pl.when(end)
    def _():
        pl.semaphore_wait(barrier, 4)

    def token(b):
        return pl.ds(b * length, length)

    def z_own(k):
        return remote(
            gated_t, cls.at[z, :, token(0)], zs.at[k], zr.at[z], dev_in if k == 0 else dev_out
        )

    def z_pass(j):
        block = cls.at[plane[j], :, token(0)]
        return remote(block, block, zs.at[j + 1], zr.at[plane[j]], dev_in if j == 2 else dev_out)

    def z_arrive(j):
        block = cls.at[plane[j], :, token(0)]
        remote(block, block, zs.at[0], zr.at[plane[j]], dev_in).wait_recv()

    quarter = cols // 4
    kept = cols - quarter

    def extra(j):
        return cls.at[plane[j], pl.ds(kept, quarter), pl.ds(length, 3 * length)]

    def e_own(k):
        block = extra(0)
        return remote(block, block, es.at[k], er.at[z], dev_in if k == 0 else dev_out)

    def e_pass(j):
        block = extra(j)
        return remote(block, block, es.at[j + 1], er.at[plane[j]], dev_in if j == 2 else dev_out)

    def e_arrive(j):
        block = extra(j)
        remote(block, block, es.at[0], er.at[plane[j]], dev_in).wait_recv()

    def b_copy(j, kind):
        p = plane[j]
        count = cols if j == 0 else kept
        rows = pl.ds(0, count)
        if kind < 2:
            src = gated_t.at[rows, :] if j == 0 else cls.at[p, rows, token(0)]
            dst = cls.at[p, rows, token(kind + 1)]
            dev = dev_x if kind == 0 else dev_y
        else:
            rows = pl.ds(0, count // 2) if kind == 2 else pl.ds(count // 2, count // 2)
            src = cls.at[p, rows, token(1 if kind == 2 else 2)]
            dst = cls.at[p, rows, token(3)]
            dev = dev_y if kind == 2 else dev_x
        return remote(src, dst, bs.at[j, kind], br.at[j, kind], dev)

    def b_first(j):
        b_copy(j, 0).start()
        b_copy(j, 1).start()

    def b_second(j):
        b_copy(j, 0).wait_recv()
        b_copy(j, 2).start()
        b_copy(j, 1).wait_recv()
        b_copy(j, 3).start()

    def b_last(j):
        b_copy(j, 2).wait_recv()
        b_copy(j, 3).wait_recv()

    hl = length // 2
    c_rows = [
        pl.ds(length, length),
        pl.ds(2 * length, length),
        pl.ds(3 * length, hl),
        pl.ds(3 * length + hl, hl),
    ]

    def c_copy(kind):
        src_rows = [pl.ds(0, length), pl.ds(0, length), pl.ds(length, hl), pl.ds(2 * length + hl, hl)]
        dev = dev_x if kind in (0, 3) else dev_y
        mine = pl.ds(0, cols)
        return remote(
            og.at[src_rows[kind], mine], og.at[c_rows[kind], mine], cs.at[kind], cr.at[kind], dev
        )

    def k_copy(kind):
        return remote(
            og.at[c_rows[kind], pl.ds(0, cols)],
            og.at[c_rows[kind], pl.ds(cols, cols)],
            ks.at[kind],
            kr.at[kind],
            dev_core,
        )

    b_first(0)

    z_own(0).start()

    @pl.when(inner)
    def _():
        z_own(1).start()

    own_cols(0, 0).wait()
    own_cols(1, 1).wait()
    c_copy(0).start()
    c_copy(1).start()
    total[...] = spread(jnp.broadcast_to(factors[0, length - 1 :, :], (8, heads)))
    total_copy = remote(total, total_x, ts.at[2], tr.at[2], dev_x)
    total_copy.start()

    def product(i, dst):
        w_load(i).wait()

        def step(r, _):
            lanes = pl.ds(pl.multiple_of(r * tile, tile), tile)
            part = lax.dot_general(
                og[pl.ds(0, length), pl.ds(0, cols)],
                wbuf[i % 2, lanes, :],
                (((1,), (1,)), ((), ())),
                preferred_element_type=f32,
            )
            dst[:, lanes] = part.astype(bf16)
            return 0

        lax.fori_loop(0, tiles, step, 0)
        if i + 2 < 8:
            w_load(i + 2).start()

    def x_copy(n):
        return remote(xsend.at[n % 2], xrecv.at[n], xs.at[n % 2], xr.at[n], dev_core)

    rows_at_once = min(64, length)

    def by_rows(body):
        def step(r, _):
            body(pl.ds(pl.multiple_of(r * rows_at_once, rows_at_once), rows_at_once))
            return 0

        lax.fori_loop(0, length // rows_at_once, step, 0)

    def add_into(n, other):
        def body(rows):
            xsum[n, rows, :] = (xsum[n, rows, :].astype(f32) + other[rows, :].astype(f32)).astype(bf16)

        by_rows(body)

    def rs_end(n):
        return remote(xsum.at[n], rs.at[n], rss.at[n], rsr.at[n], dev_in)

    def rs_inner(n):
        dst, dev = [(3, dev_in), (4, dev_in), (2, dev_out)][n]
        return remote(xsum.at[n], rs.at[dst], rss.at[n], rsr.at[dst], dev)

    def rs_arrive(slot):
        remote(rs.at[slot], rs.at[slot], rss.at[0], rsr.at[slot], dev_in).wait_recv()

    for n in range(4):
        if n >= 2:
            x_copy(n - 2).wait_send()
        product(2 * n, xsend.at[n % 2])
        x_copy(n).start()
        product(2 * n + 1, xsum.at[n])
        if n:
            x_copy(n - 1).wait_recv()
            add_into(n - 1, xrecv.at[n - 1])

            @pl.when(end)
            def _():
                rs_end(n - 1).start()

    x_copy(3).wait_recv()
    x_copy(2).wait_send()
    x_copy(3).wait_send()

    def place(r, _):
        rows = pl.ds(pl.multiple_of(r * tile, tile), tile)
        cls[z, rows, token(0)] = gated_t[rows, :]
        return 0

    lax.fori_loop(0, tiles, place, 0)

    z_arrive(1)
    b_first(1)

    @pl.when(inner)
    def _():
        z_pass(1).start()
        z_arrive(2)
        z_pass(2).start()

    b_second(0)

    @pl.when(inner)
    def _():
        rs_arrive(0)
        add_into(0, rs.at[0])
        rs_inner(0).start()

    c_copy(0).wait_recv()
    c_copy(2).start()
    k_copy(0).start()
    c_copy(1).wait_recv()
    c_copy(3).start()
    k_copy(1).start()

    @pl.when(inner)
    def _():
        z_arrive(3)
        z_pass(3).start()
        rs_arrive(1)
        add_into(1, rs.at[1])
        rs_inner(1).start()
        rs_arrive(3)
        add_into(2, rs.at[3])
        rs_inner(2).start()

    @pl.when(end)
    def _():
        z_arrive(2)

    b_first(2)
    b_last(0)
    e_own(0).start()

    @pl.when(inner)
    def _():
        e_own(1).start()

    c_copy(2).wait_recv()
    k_copy(2).start()
    c_copy(3).wait_recv()
    k_copy(3).start()
    for kind in range(4):
        k_copy(kind).wait_recv()

    grad_scale = 1.0 / math.sqrt(length * 4)
    wide = min(512, cols)

    def out_local(j, r):
        row = pl.multiple_of((plane[j] * 2 + core) * cols + r * tile, tile)
        rows = pl.ds(pl.multiple_of(r * tile, tile), tile)
        return pltpu.make_async_copy(
            wbuf.at[0, rows, :], weight_grad.at[pl.ds(row, tile), :], ol.at[r]
        )

    def out_remote(j, r):
        row = pl.multiple_of((plane[j] * 2 + core) * cols + r * tile, tile)
        rows = pl.ds(pl.multiple_of(r * tile, tile), tile)
        return remote(
            wbuf.at[1, rows, :], weight_grad.at[pl.ds(row, tile), :], os_.at[r], or_.at[j, r], dev_core
        )

    def out_arrive(j, r):
        row = pl.multiple_of((plane[j] * 2 + 1 - core) * cols + r * tile, tile)
        there = weight_grad.at[pl.ds(row, tile), :]
        remote(there, there, os_.at[r], or_.at[j, r], dev_core).wait_recv()

    def rows_of(j):
        def step(r, _):
            rows = pl.ds(pl.multiple_of(r * tile, tile), tile)
            if j:
                out_local(j - 1, r).wait()
                out_remote(j - 1, r).wait_send()
            for n in range(2 * cols // wide):
                part = jnp.dot(
                    cls[plane[j], rows, :],
                    og[:, pl.ds(n * wide, wide)],
                    preferred_element_type=f32,
                )
                at = n * wide
                wbuf[at // cols, rows, pl.ds(at % cols, wide)] = (part * grad_scale).astype(bf16)
            out_local(j, r).start()
            out_remote(j, r).start()
            return 0

        lax.fori_loop(0, tiles, step, 0)

    rows_of(0)

    rs_arrive(2)

    @pl.when(inner)
    def _():
        rs_arrive(4)

    def top(rows):
        up = xsum[3, rows, :].astype(f32) + xrecv[3, rows, :].astype(f32) + rs[2, rows, :].astype(f32)
        up = jnp.where(inner, up + rs[4, rows, :].astype(f32), up)
        gate = gate_input[rows, :].astype(f32)
        sig = 1.0 / (1.0 + jnp.exp(-gate))
        saved = scan_output[rows, :].astype(f32)
        gate_grad[rows, :] = (up * saved * sig * (1.0 + gate * (1.0 - sig))).astype(bf16)
        grad = (up * (gate * sig)).astype(bf16)
        xsend[1, rows, :] = grad
        xsend[0, rows, :] = (grad.astype(f32) * spread(factors[0, rows, :])).astype(bf16)

    by_rows(top)
    st_own[...] = jnp.dot(out_group_t[...], xsend[0], preferred_element_type=f32).astype(bf16)
    hop_x = remote(st_own, st_x, ts.at[0], tr.at[0], dev_x)
    hop_x.start()

    def inside_of(j):
        rows = pl.ds(j * sub, sub)
        scores = jnp.dot(
            in_group[rows, :], out_group_t[:, j * sub : (j + 1) * sub], preferred_element_type=f32
        )
        at_t = lax.broadcasted_iota(jnp.int32, (sub, sub), 0)
        at_s = lax.broadcasted_iota(jnp.int32, (sub, sub), 1)
        scores = jnp.where(at_t <= at_s, scores, 0.0)
        left = lax.broadcasted_iota(jnp.int32, (sub, 2 * width), 1) < width
        for pair in range(heads // 2):
            lanes = pl.ds(pair * 2 * width, 2 * width)
            grads = xsend[1, rows, lanes]
            sums = []
            for head in (2 * pair, 2 * pair + 1):
                ahead = cumul_t[head : head + 1, j * sub : (j + 1) * sub] - cumul[rows, head : head + 1]
                weights = (scores * jnp.exp(jnp.minimum(ahead, 0.0))).astype(bf16)
                sums.append(jnp.dot(weights, grads, preferred_element_type=f32))
            inside[rows, lanes] = jnp.where(left, sums[0], sums[1])
        if j < 3:
            seen = jnp.dot(in_group[rows, :], state[...].astype(bf16), preferred_element_type=f32)
            inside[rows, :] += seen * spread(factors[2, rows, :])
        if j:
            decay = spread(factors[1, rows, :])
            fresh = jnp.dot(
                out_group_t[:, j * sub : (j + 1) * sub],
                (xsend[1, rows, :].astype(f32) * decay).astype(bf16),
                preferred_element_type=f32,
            )
            state[...] = fresh if j == 3 else fresh + decay[sub - 1 :, :] * state[...]

    def finish_rows(j):
        rows = pl.ds(j * sub, sub)
        seen = jnp.dot(in_group[rows, :], st_own[...], preferred_element_type=f32)
        grad = xsend[1, rows, :].astype(f32)
        input_grad[rows, :] = (
            spread(factors[4, rows, :]) * (inside[rows, :] + spread(factors[3, rows, :]) * seen)
            + skip[0:1, :] * grad
        ).astype(bf16)

    b_second(1)

    @pl.when(end)
    def _():
        z_arrive(3)

    b_first(3)

    @pl.when(inner)
    def _():
        e_arrive(1)
        e_pass(1).start()
        e_arrive(2)
        e_pass(2).start()

    inside_of(3)
    inside_of(2)
    total_copy.wait_recv()
    hop_x.wait_recv()
    hop_y = remote(st_pair, st_y, ts.at[1], tr.at[1], dev_y)
    mine, theirs = st_own[...].astype(f32), st_x[...].astype(f32)
    st_pair[...] = jnp.where(
        s == 2, mine + total[0:1, :] * theirs, theirs + total_x[0:1, :] * mine
    ).astype(bf16)

    @pl.when(s >= 2)
    def _():
        hop_y.start()

    b_second(2)

    @pl.when(end)
    def _():
        e_arrive(1)

    b_last(1)
    rows_of(1)

    @pl.when(inner)
    def _():
        e_arrive(3)
        e_pass(3).start()

    hop_x.wait_send()

    @pl.when(s < 2)
    def _():
        hop_y.wait_recv()
        later = st_y[...].astype(f32)
        st_own[...] = jnp.where(
            s == 0, st_x[...].astype(f32) + total_x[0:1, :] * later, later
        ).astype(bf16)

    @pl.when(s >= 2)
    def _():
        st_own[...] = jnp.where(s == 2, st_x[...].astype(f32), 0.0).astype(bf16)

    inside_of(1)
    inside_of(0)
    b_second(3)

    @pl.when(end)
    def _():
        e_arrive(2)

    b_last(2)
    rows_of(2)
    for j in range(4):
        finish_rows(j)
    b_last(3)

    @pl.when(end)
    def _():
        e_arrive(3)

    rows_of(3)

    for j in range(4):
        for kind in range(4):
            b_copy(j, kind).wait_send()
    for kind in range(4):
        c_copy(kind).wait_send()
        k_copy(kind).wait_send()
    total_copy.wait_send()

    @pl.when(s >= 2)
    def _():
        hop_y.wait_send()

    z_own(0).wait_send()
    e_own(0).wait_send()
    for n in range(3):
        rs_end(n).wait_send()

    @pl.when(inner)
    def _():
        z_own(1).wait_send()
        e_own(1).wait_send()
        for j in (1, 2, 3):
            z_pass(j).wait_send()
            e_pass(j).wait_send()

    def drain(r, _):
        out_local(3, r).wait()
        out_remote(3, r).wait_send()
        for j in range(4):
            out_arrive(j, r)
        return 0

    lax.fori_loop(0, tiles, drain, 0)


def scan_factors(cumul, step_size):
    length = cumul.shape[0]
    sub = length // 4
    ends = cumul[sub - 1 :: sub]
    zero = jnp.zeros_like(ends[:1])
    before = jnp.repeat(jnp.concatenate([zero, ends[:-1]]), sub, axis=0)
    after = jnp.repeat(ends, sub, axis=0)
    fades = [cumul, cumul - before, after - cumul, ends[-1:] - cumul]
    return jnp.stack([jnp.exp(f) for f in fades] + [step_size])


def call_exchange(
    out_grad, out_weight, gated_t, gate_input, scan_output, in_group, out_group_t, factors, cumul, skip
):
    cols, length = gated_t.shape
    state = out_group_t.shape[0]
    heads = cumul.shape[1]
    tiles = cols // min(256, cols)
    dma = pltpu.SemaphoreType.DMA
    hbm = pl.BlockSpec(memory_space=pl.ANY)
    vmem = pl.BlockSpec(memory_space=pltpu.VMEM)
    owner = jnp.arange(cols) // (cols // heads)
    expand = (owner[None, :] == jnp.arange(heads)[:, None]).astype(f32)
    skip = jnp.broadcast_to(jnp.repeat(skip, cols // heads)[None], (8, cols))
    return pl.pallas_call(
        exchange,
        out_shape=(
            jax.ShapeDtypeStruct(out_weight.shape, bf16),
            jax.ShapeDtypeStruct((length, cols), bf16),
            jax.ShapeDtypeStruct((length, cols), bf16),
        ),
        in_specs=[hbm, hbm] + [vmem] * 10,
        out_specs=(hbm, vmem, vmem),
        scratch_shapes=[
            pltpu.VMEM((4, cols, 4 * length), bf16),
            pltpu.VMEM((4 * length, 2 * cols), bf16),
            pltpu.VMEM((2, cols, cols), bf16),
            pltpu.VMEM((2, length, cols), bf16),
            pltpu.VMEM((4, length, cols), bf16),
            pltpu.VMEM((4, length, cols), bf16),
            pltpu.VMEM((5, length, cols), bf16),
            pltpu.VMEM((state, cols), bf16),
            pltpu.VMEM((state, cols), bf16),
            pltpu.VMEM((state, cols), bf16),
            pltpu.VMEM((state, cols), bf16),
            pltpu.VMEM((8, cols), f32),
            pltpu.VMEM((8, cols), f32),
            pltpu.VMEM((length, cols), f32),
            pltpu.VMEM((state, cols), f32),
            dma((2,)),
            dma((2,)),
            dma((2,)),
            dma((4,)),
            dma((3,)),
            dma((5,)),
            dma((5,)),
            dma((4,)),
            dma((5,)),
            dma((4,)),
            dma((4, 4)),
            dma((4, 4)),
            dma((4,)),
            dma((4,)),
            dma((4,)),
            dma((4,)),
            dma((3,)),
            dma((3,)),
            dma((tiles,)),
            dma((tiles,)),
            dma((4, tiles)),
        ],
        compiler_params=pltpu.CompilerParams(
            collective_id=0, has_side_effects=True, vmem_limit_bytes=63 * 1024 * 1024
        ),
    )(
        out_grad,
        out_weight,
        gated_t,
        gate_input,
        scan_output,
        in_group,
        out_group_t,
        factors,
        cumul,
        cumul.T,
        expand,
        skip,
    )


def routed(
    out_grad,
    out_weight,
    gate_input,
    scan_output,
    step_size,
    log_decay,
    input_map,
    output_map,
    skip_gain,
):
    _, _, gated = gate_terms(gate_input, scan_output)
    in_group, out_group = group_maps(input_map, output_map, log_decay.shape[1])
    cumul = jnp.cumsum(log_decay, axis=0)
    weight_grad, gate_grad, input_grad = call_exchange(
        out_grad,
        out_weight,
        gated.T,
        gate_input,
        scan_output,
        in_group,
        out_group.T,
        scan_factors(cumul, step_size),
        cumul,
        skip_gain,
    )
    return input_grad, gate_grad, weight_grad


def solution(mesh):
    in_specs = (
        P("seq", None),
        P(None, "head"),
        P("seq", "head"),
        P("seq", "head"),
        P("seq", "head"),
        P("seq", "head"),
        P("seq", None, None),
        P("seq", None, None),
        P("head"),
    )
    out_specs = (P("seq", "head"), P("seq", "head"), P(None, "head"))
    small = mesh.shape["seq"] == 4 and mesh.shape["head"] == 8
    return jax.shard_map(
        routed if small else general,
        mesh=mesh,
        in_specs=in_specs,
        out_specs=out_specs,
        check_vma=False,
    )
```

profile of v0, /device:TPU:0, one launch (start us, length us, event | category | flops | bytes accessed | tf_op | source)
XLA Modules:
  0.0 215.8 jit_solution(3883949112821205775)
XLA Ops:
  0.6 0.0 copy-start
  0.7 0.7 broadcast_in_dim.20
  1.4 0.1 broadcast_in_dim.21
  1.5 0.6 broadcast_in_dim.22.skip
  2.1 1.1 reduce-window.6
  3.2 0.2 slice_reduce_fusion
  3.4 0.6 fusion.6.expand
  4.1 0.7 copy_bitcast_fusion.1
  4.7 0.1 slice.17
  4.8 0.2 slice_reduce_fusion.1
  5.0 0.1 concatenate.3
  5.1 0.1 broadcast_in_dim.18
  5.2 0.1 broadcast_in_dim.19
  5.2 0.1 bitcast_dynamic-update-slice_fusion.2
  5.3 0.1 fusion.12
  5.4 0.0 copy-start.2
  5.4 0.1 fusion.9
  5.5 0.1 bitcast_dynamic-update-slice_fusion.1
  5.6 0.9 bitcast_dynamic-update-slice_fusion
  6.5 0.8 copy.26.cumul
  7.3 2.6 %constant_dynamic-slice_fusion = (bf16[512,1,256]{2,1,0:T(2,128)(2,1)S(1)}, bf16[512,1,256]{2,1,0:T(2,128)(2,1)S(1)}) fusion(bf16[512,4,256]{2,1,0:T(4,128)(2,1)} %param.16, s32[]{:T(128)S(6)} %select_n.20, bf16[512,4,256]{2,1,0:T(4,128)(2,1)} %param.15), kind=kLoop, calls=%fused_computation.34 | loop fusion | bytes 1048580 | tf_op jit(solution)/shard_map/jit(dynamic_index_in_dim)/dynamic_slice | solution.py:80
  10.0 0.0 copy-start.3
  10.0 1.3 copy.22
  11.3 0.7 copy.47
  12.0 0.5 copy.20
  12.6 0.5 copy.19
  13.1 1.6 fusion.5.gated_t
  14.8 1.5 copy.25.factors
  16.2 182.3 %shard_map.112 = (bf16[8192,1024]{1,0:T(8,128)(2,1)}, bf16[512,1024]{1,0:T(8,128)(2,1)}, bf16[512,1024]{1,0:T(8,128)(2,1)}) custom-call(bf16[512,8192]{1,0:T(8,128)(2,1)} %out_grad.1, bf16[8192,1024]{1,0:T(8,128)(2,1)} %out_weight.1, bf16[1024,512]{1,0:T(8,128)(2,1)} %fusion.5.gated_t, bf16[512,1024]{1,0:T(8,128)(2,1)} %gate_input.1, ...), custom_call_target="tpu_custom_call" | custom-call | tf_op jit(solution)/shard_map/pallas_call | solution.py:728
  198.5 2.4 %copy.55 = bf16[512,1024]{1,0:T(8,128)(2,1)} copy(bf16[512,1024]{1,0:T(8,128)(2,1)} %get-tuple-element.16) | data formatting | bytes 2097152
  200.9 1.0 copy.56
  201.9 13.9 %copy.57 = bf16[8192,1024]{1,0:T(8,128)(2,1)} copy(bf16[8192,1024]{1,0:T(8,128)(2,1)} %get-tuple-element.18) | data formatting | bytes 33554432
  (11 shorter events, 0.1 us)
Async XLA Ops:
  0.6 1.5 copy-start
  5.4 6.6 %copy-start.2 = (bf16[512,1024]{1,0:T(8,128)(2,1)S(1)}, bf16[512,1024]{1,0:T(8,128)(2,1)}, u32[]{:S(2)}) copy-start(bf16[512,1024]{1,0:T(8,128)(2,1)} %gate_input.1) | copy-start | bytes 3145732
  10.0 2.6 %copy-start.3 = (bf16[512,1024]{1,0:T(8,128)(2,1)S(1)}, bf16[512,1024]{1,0:T(8,128)(2,1)}, u32[]{:S(2)}) copy-start(bf16[512,1024]{1,0:T(8,128)(2,1)} %scan_output.1) | copy-start | bytes 3145732
  198.5 2.4 %copy-start.4 = (bf16[512,1024]{1,0:T(8,128)(2,1)S(1)}, bf16[512,1024]{1,0:T(8,128)(2,1)}, u32[]{:S(2)}) copy-start(bf16[512,1024]{1,0:T(8,128)(2,1)} %get-tuple-element.17) | copy-start | bytes 3145732
  201.9 13.9 %copy-start.1 = (f32[512,16]{0,1:T(8,128)S(1)}, f32[512,16]{0,1:T(8,128)}, u32[]{:S(2)}) copy-start(f32[512,16]{0,1:T(8,128)} %param.14) | copy-start | bytes 98308
where the time goes:
time: 216 us
  Pallas kernels  182 us (84%)
  local copies, waits for them, and re-layouts  28.3 us (13%)
  other arithmetic  4.46 us (2%)
    pallas_call x1, Pallas kernels, call_exchange(): pl.pallas_call(exchange, out_shape=(jax.ShapeDtypeStruct(out_weight.shape...  182 us
    unnamed x16, local copies, waits for them, and re-layouts  19.1 us

commit v1 on v0

--- a/solution.py
+++ b/solution.py
@@ -139,16 +139,13 @@
 def exchange(
     out_grad,
     out_weight,
-    gated_t,
     gate_input,
     scan_output,
     in_group,
     out_group_t,
-    factors,
-    cumul,
-    cumul_t,
-    expand,
-    skip,
+    log_decay_t,
+    step_t,
+    skip_gain,
     weight_grad,
     gate_grad,
     input_grad,
@@ -167,6 +164,10 @@
     total_x,
     inside,
     state,
+    factors,
+    cumul,
+    cumul_t,
+    expand,
     local_sem,
     w_sem,
     xs,
@@ -189,9 +190,9 @@
     os_,
     or_,
 ):
-    cols, length = gated_t.shape
-    tile = min(256, cols)
-    tiles = cols // tile
+    length, cols = gate_input.shape
+    tiles = 4
+    tile = cols // tiles
     s, h = lax.axis_index("seq"), lax.axis_index("head")
     z, core = lax.div(h, 2), lax.rem(h, 2)
     upper = lax.div(z, 2)
@@ -212,7 +213,7 @@
             src_ref=src, dst_ref=dst, send_sem=ssem, recv_sem=rsem, device_id=dev, device_id_type=MESH
         )
 
-    heads = cumul.shape[1]
+    heads = log_decay_t.shape[0]
     width = cols // heads
     sub = length // 4
 
@@ -239,6 +240,16 @@
     w_load(0).start()
     w_load(1).start()
 
+    def place(r, _):
+        at = pl.ds(pl.multiple_of(r * tile, tile), tile)
+        gate = gate_input[:, at].astype(f32)
+        saved = scan_output[:, at].astype(f32)
+        gated = saved * (gate / (1.0 + jnp.exp(-gate)))
+        cls[z, at, 0:length] = jnp.transpose(gated).astype(bf16)
+        return 0
+
+    lax.fori_loop(0, tiles, place, 0)
+
     barrier = pltpu.get_barrier_semaphore()
     for dev in (dev_core, dev_x, dev_y, dev_in):
         pl.semaphore_signal(barrier, inc=1, device_id=dev, device_id_type=MESH)
@@ -260,7 +271,7 @@
 
     def z_own(k):
         return remote(
-            gated_t, cls.at[z, :, token(0)], zs.at[k], zr.at[z], dev_in if k == 0 else dev_out
+            cls.at[z, :, token(0)], cls.at[z, :, token(0)], zs.at[k], zr.at[z], dev_in if k == 0 else dev_out
         )
 
     def z_pass(j):
@@ -294,7 +305,7 @@
         count = cols if j == 0 else kept
         rows = pl.ds(0, count)
         if kind < 2:
-            src = gated_t.at[rows, :] if j == 0 else cls.at[p, rows, token(0)]
+            src = cls.at[p, rows, token(0)]
             dst = cls.at[p, rows, token(kind + 1)]
             dev = dev_x if kind == 0 else dev_y
         else:
@@ -355,9 +366,43 @@
     own_cols(1, 1).wait()
     c_copy(0).start()
     c_copy(1).start()
-    total[...] = spread(jnp.broadcast_to(factors[0, length - 1 :, :], (8, heads)))
     total_copy = remote(total, total_x, ts.at[2], tr.at[2], dev_x)
-    total_copy.start()
+
+    def gather_factors():
+        at_t = lax.broadcasted_iota(jnp.int32, (length, length), 0)
+        at_s = lax.broadcasted_iota(jnp.int32, (length, length), 1)
+        upto = (at_s <= at_t).astype(f32)
+        from_on = (at_t <= at_s).astype(f32)
+        same = (at_t == at_s).astype(f32)
+
+        def by_token(matrix, values):
+            return lax.dot_general(
+                matrix,
+                values,
+                (((1,), (1,)), ((), ())),
+                precision=highest,
+                preferred_element_type=f32,
+            )
+
+        cumul[...] = by_token(upto, log_decay_t[...])
+        cumul_t[...] = jnp.dot(
+            log_decay_t[...], from_on, precision=highest, preferred_element_type=f32
+        )
+        factors[4, :, :] = by_token(same, step_t[...])
+        first = lax.broadcasted_iota(jnp.int32, (heads, cols), 0) * width
+        lane = lax.broadcasted_iota(jnp.int32, (heads, cols), 1)
+        expand[...] = ((lane >= first) & (lane < first + width)).astype(f32)
+        last = cumul[length - 1 :, :]
+        for j in range(4):
+            rows = pl.ds(j * sub, sub)
+            here = cumul[rows, :]
+            end_here = cumul[(j + 1) * sub - 1 : (j + 1) * sub, :]
+            before = cumul[j * sub - 1 : j * sub, :] if j else jnp.zeros_like(last)
+            factors[0, rows, :] = jnp.exp(here)
+            factors[1, rows, :] = jnp.exp(here - before)
+            factors[2, rows, :] = jnp.exp(end_here - here)
+            factors[3, rows, :] = jnp.exp(last - here)
+        total[...] = spread(jnp.broadcast_to(jnp.exp(last), (8, heads)))
 
     def product(i, dst):
         w_load(i).wait()
@@ -423,12 +468,8 @@
     x_copy(2).wait_send()
     x_copy(3).wait_send()
 
-    def place(r, _):
-        rows = pl.ds(pl.multiple_of(r * tile, tile), tile)
-        cls[z, rows, token(0)] = gated_t[rows, :]
-        return 0
-
-    lax.fori_loop(0, tiles, place, 0)
+    gather_factors()
+    total_copy.start()
 
     z_arrive(1)
     b_first(1)
@@ -506,25 +547,52 @@
         there = weight_grad.at[pl.ds(row, tile), :]
         remote(there, there, os_.at[r], or_.at[j, r], dev_core).wait_recv()
 
-    def rows_of(j):
+    early = 3 * length
+
+    def held_at(part, r):
+        per = length // tile
+        row = pl.multiple_of(lax.rem(r, per) * tile, tile)
+        return part * 2 + lax.div(r, per), pl.ds(row, tile)
+
+    def early_rows():
+        def step(r, _):
+            rows = pl.ds(pl.multiple_of(r * tile, tile), tile)
+            for n in range(2 * cols // wide):
+                part = jnp.dot(
+                    cls[plane[3], rows, pl.ds(0, early)],
+                    og[pl.ds(0, early), pl.ds(n * wide, wide)],
+                    preferred_element_type=f32,
+                )
+                slab, at_rows = held_at(n * wide // cols, r)
+                xsum[slab, at_rows, pl.ds(n * wide % cols, wide)] = part.astype(bf16)
+            return 0
+
+        lax.fori_loop(0, tiles - 1, step, 0)
+
+    def rows_of(j, first=0, last=4, begun=False):
         def step(r, _):
             rows = pl.ds(pl.multiple_of(r * tile, tile), tile)
             if j:
                 out_local(j - 1, r).wait()
                 out_remote(j - 1, r).wait_send()
             for n in range(2 * cols // wide):
+                at = n * wide
+                lanes = pl.ds(at % cols, wide)
+                tokens = pl.ds(early, length) if begun else pl.ds(0, 4 * length)
                 part = jnp.dot(
-                    cls[plane[j], rows, :],
-                    og[:, pl.ds(n * wide, wide)],
+                    cls[plane[j], rows, tokens],
+                    og[tokens, pl.ds(at, wide)],
                     preferred_element_type=f32,
                 )
-                at = n * wide
-                wbuf[at // cols, rows, pl.ds(at % cols, wide)] = (part * grad_scale).astype(bf16)
+                if begun:
+                    slab, at_rows = held_at(at // cols, r)
+                    part = part + xsum[slab, at_rows, lanes].astype(f32)
+                wbuf[at // cols, rows, lanes] = (part * grad_scale).astype(bf16)
             out_local(j, r).start()
             out_remote(j, r).start()
             return 0
 
-        lax.fori_loop(0, tiles, step, 0)
+        lax.fori_loop(first, last, step, 0)
 
     rows_of(0)
 
@@ -581,6 +649,7 @@
             state[...] = fresh if j == 3 else fresh + decay[sub - 1 :, :] * state[...]
 
     def finish_rows(j):
+        skip = spread(jnp.broadcast_to(skip_gain[...], (8, heads)))
         rows = pl.ds(j * sub, sub)
         seen = jnp.dot(in_group[rows, :], st_own[...], preferred_element_type=f32)
         grad = xsend[1, rows, :].astype(f32)
@@ -658,13 +727,17 @@
     rows_of(2)
     for j in range(4):
         finish_rows(j)
+    for n in range(3):
+        rs_end(n).wait_send()
+    early_rows()
     b_last(3)
+    rows_of(3, 0, tiles - 1, True)
 
     @pl.when(end)
     def _():
         e_arrive(3)
 
-    rows_of(3)
+    rows_of(3, tiles - 1, tiles)
 
     for j in range(4):
         for kind in range(4):
@@ -680,8 +753,6 @@
 
     z_own(0).wait_send()
     e_own(0).wait_send()
-    for n in range(3):
-        rs_end(n).wait_send()
 
     @pl.when(inner)
     def _():
@@ -701,30 +772,16 @@
     lax.fori_loop(0, tiles, drain, 0)
 
 
-def scan_factors(cumul, step_size):
-    length = cumul.shape[0]
-    sub = length // 4
-    ends = cumul[sub - 1 :: sub]
-    zero = jnp.zeros_like(ends[:1])
-    before = jnp.repeat(jnp.concatenate([zero, ends[:-1]]), sub, axis=0)
-    after = jnp.repeat(ends, sub, axis=0)
-    fades = [cumul, cumul - before, after - cumul, ends[-1:] - cumul]
-    return jnp.stack([jnp.exp(f) for f in fades] + [step_size])
-
-
 def call_exchange(
-    out_grad, out_weight, gated_t, gate_input, scan_output, in_group, out_group_t, factors, cumul, skip
+    out_grad, out_weight, gate_input, scan_output, in_group, out_group_t, log_decay, step_size, skip
 ):
-    cols, length = gated_t.shape
+    length, cols = gate_input.shape
     state = out_group_t.shape[0]
-    heads = cumul.shape[1]
-    tiles = cols // min(256, cols)
+    heads = log_decay.shape[1]
+    tiles = 4
     dma = pltpu.SemaphoreType.DMA
     hbm = pl.BlockSpec(memory_space=pl.ANY)
     vmem = pl.BlockSpec(memory_space=pltpu.VMEM)
-    owner = jnp.arange(cols) // (cols // heads)
-    expand = (owner[None, :] == jnp.arange(heads)[:, None]).astype(f32)
-    skip = jnp.broadcast_to(jnp.repeat(skip, cols // heads)[None], (8, cols))
     return pl.pallas_call(
         exchange,
         out_shape=(
@@ -732,7 +789,7 @@
             jax.ShapeDtypeStruct((length, cols), bf16),
             jax.ShapeDtypeStruct((length, cols), bf16),
         ),
-        in_specs=[hbm, hbm] + [vmem] * 10,
+        in_specs=[hbm, hbm] + [vmem] * 7,
         out_specs=(hbm, vmem, vmem),
         scratch_shapes=[
             pltpu.VMEM((4, cols, 4 * length), bf16),
@@ -750,6 +807,10 @@
             pltpu.VMEM((8, cols), f32),
             pltpu.VMEM((length, cols), f32),
             pltpu.VMEM((state, cols), f32),
+            pltpu.VMEM((5, length, heads), f32),
+            pltpu.VMEM((length, heads), f32),
+            pltpu.VMEM((heads, length), f32),
+            pltpu.VMEM((heads, cols), f32),
             dma((2,)),
             dma((2,)),
             dma((2,)),
@@ -778,16 +839,13 @@
     )(
         out_grad,
         out_weight,
-        gated_t,
         gate_input,
         scan_output,
         in_group,
         out_group_t,
-        factors,
-        cumul,
-        cumul.T,
-        expand,
-        skip,
+        log_decay.T,
+        step_size.T,
+        skip[None, :],
     )
 
 
@@ -802,19 +860,16 @@
     output_map,
     skip_gain,
 ):
-    _, _, gated = gate_terms(gate_input, scan_output)
     in_group, out_group = group_maps(input_map, output_map, log_decay.shape[1])
-    cumul = jnp.cumsum(log_decay, axis=0)
     weight_grad, gate_grad, input_grad = call_exchange(
         out_grad,
         out_weight,
-        gated.T,
         gate_input,
         scan_output,
         in_group,
         out_group.T,
-        scan_factors(cumul, step_size),
-        cumul,
+        log_decay,
+        step_size,
         skip_gain,
     )
     return input_grad, gate_grad, weight_grad

time: 216 us -> 207 us (0.958)
  local copies, waits for them, and re-layouts: 28.3 us -> 23.1 us
  other arithmetic: 4.46 us -> 0 us
    another operation x4 -> x0, local copies, waits for them, and re-layouts: 3.17 us -> none  [the longest x2 2.33 us: scan_factors(): return jnp.stack([jnp.exp(f) for f in fades] + [step_size])]
    unnamed x16 -> x4, local copies, waits for them, and re-layouts: 19.1 us -> 19.2 us
where the time goes in v1:
time: 207 us
  Pallas kernels  183 us (88%)
  local copies, waits for them, and re-layouts  23.1 us (11%)
    pallas_call x1, Pallas kernels, call_exchange(): pl.pallas_call(exchange, out_shape=(jax.ShapeDtypeStruct(out_weight.shape...  183 us
    unnamed x4, local copies, waits for them, and re-layouts  19.2 us

profile of v1, /device:TPU:0, one launch (start us, length us, event | category | flops | bytes accessed | tf_op | source)
XLA Modules:
  0.0 207.1 jit_solution(7233348259924815222)
XLA Ops:
  0.6 2.6 %constant_dynamic-slice_fusion = (bf16[512,1,256]{2,1,0:T(2,128)(2,1)S(1)}, bf16[512,1,256]{2,1,0:T(2,128)(2,1)S(1)}) fusion(bf16[512,4,256]{2,1,0:T(4,128)(2,1)} %param.16, s32[]{:T(128)S(6)} %select_n.11, bf16[512,4,256]{2,1,0:T(4,128)(2,1)} %param.15), kind=kLoop, calls=%fused_computation.1 | loop fusion | bytes 1048580 | tf_op jit(solution)/shard_map/jit(dynamic_index_in_dim)/dynamic_slice | solution.py:80
  3.3 1.3 copy.14
  4.6 0.7 copy.17
  5.3 183.3 %shard_map.112 = (bf16[8192,1024]{1,0:T(8,128)(2,1)}, bf16[512,1024]{1,0:T(8,128)(2,1)}, bf16[512,1024]{1,0:T(8,128)(2,1)}) custom-call(bf16[512,8192]{1,0:T(8,128)(2,1)} %out_grad.1, bf16[8192,1024]{1,0:T(8,128)(2,1)} %out_weight.1, bf16[512,1024]{1,0:T(8,128)(2,1)} %gate_input.1, bf16[512,1024]{1,0:T(8,128)(2,1)} %scan_output.1, ...), custom_call_target="tpu_custom_call" | custom-call | tf_op jit(solution)/shard_map/pallas_call | solution.py:785
  188.7 2.3 %copy.21 = bf16[512,1024]{1,0:T(8,128)(2,1)} copy(bf16[512,1024]{1,0:T(8,128)(2,1)} %get-tuple-element.14) | data formatting | bytes 2097152
  190.9 2.3 %copy.22 = bf16[512,1024]{1,0:T(8,128)(2,1)} copy(bf16[512,1024]{1,0:T(8,128)(2,1)} %get-tuple-element.15) | data formatting | bytes 2097152
  193.2 13.9 %copy.23 = bf16[8192,1024]{1,0:T(8,128)(2,1)} copy(bf16[8192,1024]{1,0:T(8,128)(2,1)} %get-tuple-element.16) | data formatting | bytes 33554432

commit v2 on v1

--- a/solution.py
+++ b/solution.py
@@ -522,6 +522,7 @@
     k_copy(2).start()
     c_copy(3).wait_recv()
     k_copy(3).start()
+    b_second(1)
     for kind in range(4):
         k_copy(kind).wait_recv()
 
@@ -595,6 +596,12 @@
         lax.fori_loop(first, last, step, 0)
 
     rows_of(0)
+
+    @pl.when(end)
+    def _():
+        z_arrive(3)
+
+    b_first(3)
 
     rs_arrive(2)
 
@@ -658,13 +665,9 @@
             + skip[0:1, :] * grad
         ).astype(bf16)
 
-    b_second(1)
-
-    @pl.when(end)
-    def _():
-        z_arrive(3)
-
-    b_first(3)
+    inside_of(3)
+    b_second(2)
+    inside_of(2)
 
     @pl.when(inner)
     def _():
@@ -673,8 +676,6 @@
         e_arrive(2)
         e_pass(2).start()
 
-    inside_of(3)
-    inside_of(2)
     total_copy.wait_recv()
     hop_x.wait_recv()
     hop_y = remote(st_pair, st_y, ts.at[1], tr.at[1], dev_y)
@@ -687,20 +688,21 @@
     def _():
         hop_y.start()
 
-    b_second(2)
-
     @pl.when(end)
     def _():
         e_arrive(1)
 
     b_last(1)
     rows_of(1)
+    b_second(3)
 
     @pl.when(inner)
     def _():
         e_arrive(3)
         e_pass(3).start()
 
+    inside_of(1)
+    inside_of(0)
     hop_x.wait_send()
 
     @pl.when(s < 2)
@@ -714,10 +716,6 @@
     @pl.when(s >= 2)
     def _():
         st_own[...] = jnp.where(s == 2, st_x[...].astype(f32), 0.0).astype(bf16)
-
-    inside_of(1)
-    inside_of(0)
-    b_second(3)
 
     @pl.when(end)
     def _():
@@ -770,6 +768,47 @@
         return 0
 
     lax.fori_loop(0, tiles, drain, 0)
+
+
+def hand_on(wide_in, gate_in, input_in, wide_out, gate_out, input_out, wide, small, in_sem, out_sem):
+    pieces, rows, _ = wide.shape
+    moves = [
+        (wide_in.at[pl.ds(n * rows, rows), :], wide.at[n], wide_out.at[pl.ds(n * rows, rows), :])
+        for n in range(pieces)
+    ] + [(gate_in, small.at[0], gate_out), (input_in, small.at[1], input_out)]
+    arrive = [
+        pltpu.make_async_copy(src, held, in_sem.at[n]) for n, (src, held, _) in enumerate(moves)
+    ]
+    leave = [
+        pltpu.make_async_copy(held, dst, out_sem.at[n]) for n, (_, held, dst) in enumerate(moves)
+    ]
+    for copy in arrive:
+        copy.start()
+    for copy, onward in zip(arrive, leave):
+        copy.wait()
+        onward.start()
+    for onward in leave:
+        onward.wait()
+
+
+def call_hand_on(weight_grad, gate_grad, input_grad):
+    pieces = 16
+    rows, cols = weight_grad.shape
+    hbm = pl.BlockSpec(memory_space=pl.ANY)
+    arrays = (weight_grad, gate_grad, input_grad)
+    return pl.pallas_call(
+        hand_on,
+        out_shape=tuple(jax.ShapeDtypeStruct(a.shape, a.dtype) for a in arrays),
+        in_specs=[hbm] * 3,
+        out_specs=(hbm,) * 3,
+        scratch_shapes=[
+            pltpu.VMEM((pieces, rows // pieces, cols), bf16),
+            pltpu.VMEM((2,) + gate_grad.shape, bf16),
+            pltpu.SemaphoreType.DMA((pieces + 2,)),
+            pltpu.SemaphoreType.DMA((pieces + 2,)),
+        ],
+        compiler_params=pltpu.CompilerParams(vmem_limit_bytes=60 * 1024 * 1024),
+    )(*arrays)
 
 
 def call_exchange(
@@ -782,7 +821,7 @@
     dma = pltpu.SemaphoreType.DMA
     hbm = pl.BlockSpec(memory_space=pl.ANY)
     vmem = pl.BlockSpec(memory_space=pltpu.VMEM)
-    return pl.pallas_call(
+    outs = pl.pallas_call(
         exchange,
         out_shape=(
             jax.ShapeDtypeStruct(out_weight.shape, bf16),
@@ -847,6 +886,7 @@
         step_size.T,
         skip[None, :],
     )
+    return call_hand_on(*outs)
 
 
 def routed(

time: 207 us -> 208 us (level)
  Pallas kernels: 183 us -> 202 us
  local copies, waits for them, and re-layouts: 23.1 us -> 4.69 us
    unnamed x4 -> x1, local copies, waits for them, and re-layouts: 19.2 us -> 0.74 us
    pallas_call x0 -> x1, Pallas kernels: none -> 13.8 us  [call_hand_on(): pl.pallas_call(hand_on, out_shape=tuple((jax.ShapeDtypeStruct(a.shape, a....]
    pallas_call x1, Pallas kernels: 183 us -> 188 us  [call_exchange(): pl.pallas_call(exchange, out_shape=(jax.ShapeDtypeStruct(out_weight.shape...]
where the time goes in v2:
time: 208 us
  Pallas kernels  202 us (97%)
  local copies, waits for them, and re-layouts  4.69 us (2%)
    pallas_call x1, Pallas kernels, call_exchange(): pl.pallas_call(exchange, out_shape=(jax.ShapeDtypeStruct(out_weight.shape...  188 us
    pallas_call x1, Pallas kernels, call_hand_on(): pl.pallas_call(hand_on, out_shape=tuple((jax.ShapeDtypeStruct(a.shape, a....  13.8 us

profile of v2, /device:TPU:0, one launch (start us, length us, event | category | flops | bytes accessed | tf_op | source)
XLA Modules:
  0.0 207.8 jit_solution(3098745832707516968)
XLA Ops:
  0.6 2.6 %constant_dynamic-slice_fusion = (bf16[512,1,256]{2,1,0:T(2,128)(2,1)S(1)}, bf16[512,1,256]{2,1,0:T(2,128)(2,1)S(1)}) fusion(bf16[512,4,256]{2,1,0:T(4,128)(2,1)} %param.16, s32[]{:T(128)S(6)} %select_n.11, bf16[512,4,256]{2,1,0:T(4,128)(2,1)} %param.15), kind=kLoop, calls=%fused_computation.1 | loop fusion | bytes 1048580 | tf_op jit(solution)/shard_map/jit(dynamic_index_in_dim)/dynamic_slice | solution.py:80
  3.3 1.3 copy.14
  4.6 0.7 copy.17
  5.3 188.5 %shard_map.112 = (bf16[8192,1024]{1,0:T(8,128)(2,1)}, bf16[512,1024]{1,0:T(8,128)(2,1)}, bf16[512,1024]{1,0:T(8,128)(2,1)}) custom-call(bf16[512,8192]{1,0:T(8,128)(2,1)} %out_grad.1, bf16[8192,1024]{1,0:T(8,128)(2,1)} %out_weight.1, bf16[512,1024]{1,0:T(8,128)(2,1)} %gate_input.1, bf16[512,1024]{1,0:T(8,128)(2,1)} %scan_output.1, ...), custom_call_target="tpu_custom_call" | custom-call | tf_op jit(solution)/shard_map/pallas_call | solution.py:824
  193.8 13.8 %shard_map.113 = (bf16[8192,1024]{1,0:T(8,128)(2,1)}, bf16[512,1024]{1,0:T(8,128)(2,1)}, bf16[512,1024]{1,0:T(8,128)(2,1)}) custom-call(bf16[8192,1024]{1,0:T(8,128)(2,1)} %get-tuple-element.9.wide_in, bf16[512,1024]{1,0:T(8,128)(2,1)} %get-tuple-element.10.gate_in, bf16[512,1024]{1,0:T(8,128)(2,1)} %get-tuple-element.11.input_in), custom_call_target="tpu_custom_call" | custom-call | tf_op jit(solution)/shard_map/pallas_call | solution.py:799
